TPU v7x, 32 devices: a whole 2x2x4 slice. The times are simulated.
32 devices in a mesh: store: 4 (over x, core), sku: 8 (over z, y).
Axes of the slice: x: 2, y: 2, z: 4, core: 2. Of those that a mesh axis runs over, the one named last changes fastest.
Arguments:
- base_bottom: float32 [32, 13, 4096], P(('store', 'sku')), may hold values from -6 to 6
- weight_bottom: float32 [32, 13, 4096], P(('store', 'sku')), may hold values from 0.5 to 4
- base_category: float32 [32, 13, 1024], P(('store', 'sku')), may hold values from -24 to 24
- weight_category: float32 [32, 13, 1024], P(('store', 'sku')), may hold values from 0.02 to 0.2
- base_region: float32 [32, 13, 4096], P(None, None, ('store', 'sku')), may hold values from -24 to 24
- weight_region: float32 [32, 13, 4096], P(None, None, ('store', 'sku')), may hold values from 0.02 to 0.2
- category_map: int32 [4096], replicated, may hold values from 0 to 1023
- region_map: int32 [32], replicated, may hold values from 0 to 31
Outputs:
- reconciled: float32 [32, 13, 4096], P(('store', 'sku'))
- residual: float32 [32, 13, 4096], P(('store', 'sku'))
All inputs are finite; a program needn't handle non-finite values.
Results may differ from a plain program's by a relative error of at most 0.0003.
Values sent between devices are 32-bit elements; how exact they have to be, the bound alone decides.
No kernel may reach another device: no remote copies, remote signals or barrier semaphores. Data moves between devices by JAX's collectives and lax.ppermute only.
A program may use at most 128 MiB of HBM per device.

v0:
```python
import jax
import jax.numpy as jnp
from jax import lax
from jax.experimental import pallas as pl
from jax.experimental.pallas import tpu as pltpu
from jax.sharding import Mesh
from jax.sharding import PartitionSpec as P

LANES = 128
PAD = 16
WIDE = 256
VMEM = pl.BlockSpec(memory_space=pltpu.VMEM)
HBM = pl.BlockSpec(memory_space=pltpu.HBM)
SMEM = pl.BlockSpec(memory_space=pltpu.SMEM)
FREE = pl.BlockSpec(memory_space=pltpu.VMEM)
CORES = 2


def exchange(blocks, n):
    moved = lax.all_to_all(
        blocks.reshape(n, 1, -1), ("store", "sku"), split_axis=0, concat_axis=0, tiled=True
    )
    return moved.reshape(blocks.shape)


def call(body, outs, scratch, args, specs=None, held=False, out_specs=None):
    outs = [
        out if isinstance(out, jax.ShapeDtypeStruct) else jax.ShapeDtypeStruct(out, jnp.float32)
        for out in outs
    ]
    specs = specs or [VMEM] * len(args)
    args = [
        arg if spec is SMEM or spec is FREE else pltpu.with_memory_space_constraint(arg, spec.memory_space)
        for arg, spec in zip(args, specs)
    ]
    return pl.pallas_call(
        body,
        out_shape=tuple(pltpu.VMEM(out.shape, out.dtype) if held else out for out in outs),
        in_specs=specs,
        out_specs=out_specs or tuple(VMEM for _ in outs),
        scratch_shapes=scratch,
        compiler_params=pltpu.CompilerParams(vmem_limit_bytes=24 << 20),
    )(*args)


def split(value):
    high = value.astype(jnp.bfloat16)
    return high, (value - high.astype(jnp.float32)).astype(jnp.bfloat16)


def split_all(value):
    high, low = split(value)
    rest = value - high.astype(jnp.float32) - low.astype(jnp.float32)
    return high, low, rest.astype(jnp.bfloat16)


def product(left, right, contract):
    return lax.dot_general(left, right, (contract, ((), ())), preferred_element_type=jnp.float32)


def rows_of(ref, n, h):
    return ref[pl.ds(h, n, stride=ref.shape[0] // n), :]


def put_rows(ref, n, h, value):
    ref[pl.ds(h, n, stride=ref.shape[0] // n), :] = value


def category_sums(field, table_ref, group_ref, n, rows):
    width = 4 if n % 4 == 0 else 1
    lanes = width * LANES

    def step(c, total):
        pieces = [field[pl.ds(c * width + i, PAD, stride=n), :] for i in range(width)]
        parts = split_all(jnp.concatenate(pieces, axis=1))
        start = pl.multiple_of(c * lanes, lanes)
        group = group_ref[:, pl.ds(start, lanes)]
        masks = [group == g for g in range(rows // PAD)]
        none = jnp.zeros((PAD, lanes), jnp.bfloat16)
        spread = jnp.concatenate(
            [jnp.where(mask, part, none) for part in parts for mask in masks], axis=0
        )
        return total + product(spread, table_ref[pl.ds(start, lanes), :], ((1,), (0,)))

    steps = n // width
    total = lax.fori_loop(
        0, steps, step, jnp.zeros((3 * rows, WIDE), jnp.float32), unroll=min(steps, 8)
    )
    return total[:rows] + (total[rows : 2 * rows] + total[2 * rows :])


def category_spread(values, cats, horizon, put):
    place = cats & (LANES - 1)
    group = cats >> (LANES.bit_length() - 1)
    for h in range(horizon):
        found = []
        for g in range(0, values.shape[0], PAD):
            for lane in range(0, WIDE, LANES):
                row = jnp.broadcast_to(values[g + h : g + h + 1, lane : lane + LANES], cats.shape)
                found.append(jnp.take_along_axis(row, place, axis=1))
        for bit in range((len(found) - 1).bit_length()):
            mask = group & (1 << bit) != 0
            pairs = [found[i : i + 2] for i in range(0, len(found), 2)]
            found = [jnp.where(mask, pair[1], pair[0]) if len(pair) == 2 else pair[0] for pair in pairs]
        put(h, found[0])


def tiles_of(n):
    return [slice(t, t + 8) for t in range(0, n, 8)]


def put_tile(ref, n, h, tile, value):
    rows = ref.shape[0] // n
    ref[pl.ds(tile.start * rows + h, 8, stride=rows), :] = value


def region_sums(load, same, n, horizon):
    high, low = split(jnp.concatenate([load(h) for h in range(horizon)], axis=1))
    total = product(same, high, ((1,), (0,))) + product(same, low, ((1,), (0,)))
    return [total[:, h * LANES : (h + 1) * LANES] for h in range(horizon)]


def pack_body(base_hbm, out_ref, base_ref, sem):
    copy = pltpu.make_async_copy(base_hbm, base_ref, sem)
    copy.start()
    copy.wait()
    n = base_ref.shape[1]
    for h in range(base_ref.shape[0]):
        put_rows(out_ref, n, h, base_ref[h])


def prepare_body(
    base_hbm, base_cat_hbm, weight_cat_hbm, base_reg_hbm, weight_reg_hbm, cats_hbm, map_hbm,
    spread_out, wcat_out, wstore_out, bstore_out, same_out, table_out, group_out,
    cats_ref,
    field, values, base_ref, base_cat_ref, weight_cat_ref, base_reg_ref, weight_reg_ref, map_ref, sems,
):
    copies = [
        pltpu.make_async_copy(source, target, sems.at[i])
        for i, (source, target) in enumerate(
            (
                (cats_hbm, cats_ref),
                (base_hbm, base_ref),
                (weight_cat_hbm, weight_cat_ref),
                (base_cat_hbm, base_cat_ref),
                (map_hbm, map_ref),
                (weight_reg_hbm, weight_reg_ref),
                (base_reg_hbm, base_reg_ref),
            )
        )
    ]
    for copy in copies:
        copy.start()
    for copy in copies:
        copy.wait()
    horizon, n, _ = base_ref.shape
    n_regions = weight_reg_ref.shape[1]
    square = jnp.concatenate([cats_ref[...].astype(jnp.float32)] * (LANES // min(n, LANES)), axis=0)
    labels = lax.broadcasted_iota(jnp.int32, (LANES, WIDE), 1)
    columns = [
        jnp.transpose(square[i : i + LANES]).astype(jnp.int32) % WIDE
        for i in range(0, square.shape[0], LANES)
    ]
    for j in range(n):
        column = jnp.broadcast_to(columns[j // LANES][:, j % LANES : j % LANES + 1], (LANES, WIDE))
        table_out[j * LANES : (j + 1) * LANES, :] = jnp.where(
            column == labels, 1.0, 0.0
        ).astype(jnp.bfloat16)
        group = jnp.broadcast_to(cats_ref[j : j + 1, :] // WIDE, (PAD, LANES))
        group_out[:, j * LANES : (j + 1) * LANES] = group.astype(jnp.float32).astype(jnp.bfloat16)

    field[...] = jnp.zeros_like(field)
    for h in range(horizon):
        field[h * n : (h + 1) * n, :] = base_ref[h]
    sums = category_sums(field, table_out, group_out, n, wcat_out.shape[0])
    wcat_out[...] = jnp.zeros_like(wcat_out)
    values[...] = jnp.zeros_like(values)
    for g in range(0, wcat_out.shape[0], PAD):
        for lane in range(0, WIDE, LANES):
            tile = (g // PAD * WIDE + lane) // LANES
            lanes = slice(lane, lane + LANES)
            weight = weight_cat_ref[:, tile, :]
            wcat_out[g : g + horizon, lanes] = weight
            values[g : g + horizon, lanes] = weight * (
                base_cat_ref[:, tile, :] - sums[g : g + horizon, lanes]
            )
    for tile in tiles_of(n):

        def put(h, value):
            spread_out[h, tile, :] = value

        category_spread(values, cats_ref[tile, :], horizon, put)

    labels = lax.broadcasted_iota(jnp.int32, (n_regions, n), 0)
    table = jnp.where(labels == map_ref[...], 1.0, 0.0).astype(jnp.bfloat16)
    same_out[...] = product(table, table, ((0,), (0,))).astype(jnp.bfloat16)
    for source, target in ((weight_reg_ref, wstore_out), (base_reg_ref, bstore_out)):
        for h in range(horizon):
            high, low = split(source[h])
            rest = source[h] - high.astype(jnp.float32) - low.astype(jnp.float32)
            target[h] = (
                product(table, high, ((0,), (0,)))
                + product(table, low, ((0,), (0,)))
                + product(table, rest.astype(jnp.bfloat16), ((0,), (0,)))
            )


def region_start_body(got_ref, spread_ref, wstore_ref, bstore_ref, same_ref, reg_out, send_ref):
    horizon, n, _ = spread_ref.shape
    sums = region_sums(lambda h: rows_of(got_ref, n, h), same_ref[...], n, horizon)
    for h in range(horizon):
        put_rows(send_ref, n, h, spread_ref[h])
        part = wstore_ref[h] * (bstore_ref[h] - sums[h])
        reg_out[h] = part
        put_rows(send_ref, n, horizon + h, part)


def region_part(rs, wstore_ref, same_ref, put):
    horizon, n, _ = wstore_ref.shape
    sums = region_sums(lambda h: rs[h], same_ref[...], n, horizon)
    share = jnp.zeros((n, LANES), jnp.float32)
    for h in range(horizon):
        part = wstore_ref[h] * sums[h]
        share = share + part * rs[h]
        put(h, part)
    return share


def store_part(r_ref, sums, gamma, delta, eps, diag_ref, wcat_ref, cats_ref, put, put_line, values):
    horizon, n, _ = diag_ref.shape
    scaled = wcat_ref[...] * sums
    values[...] = scaled
    square = scaled * sums
    delta = jnp.sum(delta, axis=0, keepdims=True)
    for lane in range(0, WIDE, LANES):
        delta = delta + jnp.sum(square[:, lane : lane + LANES], axis=0, keepdims=True)
    lane = lax.broadcasted_iota(jnp.int32, (1, LANES), 1)
    line = jnp.zeros((1, LANES), jnp.float32)
    for i, part in enumerate((gamma, delta, eps)):
        if part is not None:
            whole = jnp.sum(jnp.sum(part, axis=0, keepdims=True), axis=1, keepdims=True)
            line = jnp.where(lane == i, whole, line)
    put_line(jnp.broadcast_to(line, (n, LANES)))
    for tile in tiles_of(n):

        def finish(h, value):
            put(h, tile, value + diag_ref[h, tile, :] * r_ref[h, tile, :])

        category_spread(values, cats_ref[tile, :], horizon, finish)


def totals(got_ref, n, row):
    total = jnp.sum(rows_of(got_ref, n, row), axis=0, keepdims=True)
    total = jnp.broadcast_to(total, (8, LANES))
    return [
        jnp.take_along_axis(total, jnp.full((8, LANES), i, jnp.int32), axis=1)[0:1] for i in range(3)
    ]


def wide(line):
    return jnp.concatenate([line] * (WIDE // LANES), axis=1)


def region_sender(ref, n, first, keep):
    def put(h, value):
        if keep is not None:
            keep[h] = value
        put_rows(ref, n, first + h, value)

    return put


def store_sender(ref, n, keep):
    def put(h, tile, value):
        keep[h, tile, :] = value
        if ref is not None:
            put_tile(ref, n, h, tile, value)

    return put


def clear_tail(field, horizon, n):
    field[horizon * n :, :] = jnp.zeros((field.shape[0] - horizon * n, LANES), jnp.float32)


def first_body(
    a_ref, reg_ref, got_ref, diag_ref, wcat_ref, wstore_ref, table_ref, group_ref, cats_ref, same_ref,
    r_out, rs_out, cr_out, a_out, reg_out, send_ref, values, field,
):
    horizon, n, _ = diag_ref.shape
    clear_tail(field, horizon, n)
    gamma = jnp.zeros((n, LANES), jnp.float32)
    delta = jnp.zeros((n, LANES), jnp.float32)
    for h in range(horizon):
        r = a_ref[h] + rows_of(got_ref, n, horizon + h)
        r_out[h] = r
        field[h * n : (h + 1) * n, :] = r
        gamma = gamma + r * r
        delta = delta + diag_ref[h] * r * r
    sums = category_sums(field, table_ref, group_ref, n, wcat_ref.shape[0])
    cr_out[...] = sums
    for h in range(horizon):
        rs_out[h] = rows_of(got_ref, n, h) + reg_ref[h]
    delta = delta + region_part(
        rs_out, wstore_ref, same_ref, region_sender(send_ref, n, horizon, reg_out)
    )
    store_part(
        r_out, sums, gamma, delta, None, diag_ref, wcat_ref, cats_ref,
        store_sender(send_ref, n, a_out),
        lambda line: put_rows(send_ref, n, 2 * horizon, line), values,
    )


def second_body(
    a_ref, reg_ref, got_ref, x_ref, r_ref, rs_ref, cr_ref,
    diag_ref, wcat_ref, wstore_ref, table_ref, group_ref, cats_ref, same_ref,
    x_out, r_out, rs_out, s_out, ss_out, cr_out, cs_out, scal_ref, a_out, reg_out, send_ref,
    values, field,
):
    horizon, n, _ = diag_ref.shape
    clear_tail(field, horizon, n)
    for h in range(horizon):
        field[h * n : (h + 1) * n, :] = a_ref[h] + rows_of(got_ref, n, horizon + h)
    sums = category_sums(field, table_ref, group_ref, n, wcat_ref.shape[0])
    cs_out[...] = sums
    gamma, delta, _ = totals(got_ref, n, 2 * horizon)
    alpha = gamma / delta
    scal_ref[0:1, :] = gamma
    scal_ref[1:2, :] = delta
    for h in range(horizon):
        ws = rows_of(got_ref, n, h) + reg_ref[h]
        ss_out[h] = ws
        rs_out[h] = rs_ref[h] - alpha * ws
    delta = region_part(
        rs_out, wstore_ref, same_ref, region_sender(send_ref, n, horizon, reg_out)
    )
    gamma = jnp.zeros((n, LANES), jnp.float32)
    eps = jnp.zeros((n, LANES), jnp.float32)
    for h in range(horizon):
        s = field[h * n : (h + 1) * n, :]
        s_out[h] = s
        r = r_ref[h]
        x_out[h] = x_ref[h] + alpha * r
        r = r - alpha * s
        r_out[h] = r
        gamma = gamma + r * r
        delta = delta + diag_ref[h] * r * r
        eps = eps + r * s
    sums = cr_ref[...] - wide(alpha) * sums
    cr_out[...] = sums
    store_part(
        r_out, sums, gamma, delta, eps, diag_ref, wcat_ref, cats_ref,
        store_sender(send_ref, n, a_out),
        lambda line: put_rows(send_ref, n, 2 * horizon, line), values,
    )


def third_body(
    a_ref, reg_ref, got_ref, x_ref, r_ref, rs_ref, p_ref, s_ref, ss_ref, cr_ref, cs_ref, scal_ref,
    diag_ref, wcat_ref, wstore_ref, table_ref, group_ref, cats_ref, same_ref,
    x_out, r_out, p_out, s_out, scal_out, a_out, send_ref, values, field, rs_out,
):
    horizon, n, _ = diag_ref.shape
    clear_tail(field, horizon, n)
    for h in range(horizon):
        field[h * n : (h + 1) * n, :] = a_ref[h] + rows_of(got_ref, n, horizon + h)
    sums = category_sums(field, table_ref, group_ref, n, wcat_ref.shape[0])
    gamma, delta, eps = totals(got_ref, n, 2 * horizon)
    beta = gamma / scal_ref[0:1, :]
    curve = delta + 2.0 * beta * eps + beta * beta * scal_ref[1:2, :]
    alpha = gamma / curve
    scal_out[0:1, :] = gamma
    scal_out[1:2, :] = curve
    for h in range(horizon):
        ws = rows_of(got_ref, n, h) + reg_ref[h]
        rs_out[h] = rs_ref[h] - alpha * (ws + beta * ss_ref[h])
    delta = region_part(rs_out, wstore_ref, same_ref, region_sender(send_ref, n, 0, None))
    gamma = jnp.zeros((n, LANES), jnp.float32)
    eps = jnp.zeros((n, LANES), jnp.float32)
    for h in range(horizon):
        s = field[h * n : (h + 1) * n, :] + beta * s_ref[h]
        s_out[h] = s
        r = r_ref[h]
        p = r + beta * p_ref[h]
        p_out[h] = p
        x_out[h] = x_ref[h] + alpha * p
        r = r - alpha * s
        r_out[h] = r
        gamma = gamma + r * r
        delta = delta + diag_ref[h] * r * r
        eps = eps + r * s
    sums = cr_ref[...] - wide(alpha) * (sums + wide(beta) * cs_ref[...])
    store_part(
        r_out, sums, gamma, delta, eps, diag_ref, wcat_ref, cats_ref,
        store_sender(None, n, a_out), lambda line: put_rows(send_ref, n, horizon, line), values,
    )


def last_body(a_ref, got_ref, x_ref, r_ref, p_ref, s_ref, scal_ref, x_out, r_out):
    horizon, n, _ = a_ref.shape
    gamma, delta, eps = totals(got_ref, n, horizon)
    beta = gamma / scal_ref[0:1, :]
    alpha = gamma / (delta + 2.0 * beta * eps + beta * beta * scal_ref[1:2, :])
    for h in range(horizon):
        r = r_ref[h]
        s = a_ref[h] + rows_of(got_ref, n, h) + beta * s_ref[h]
        x_out[h] = x_ref[h] + alpha * (r + beta * p_ref[h])
        r_out[h] = r - alpha * s


def on_device(
    base_bottom,
    weight_bottom,
    base_category,
    weight_category,
    base_region,
    weight_region,
    category_map,
    region_map,
):
    stores, horizon, skus = base_bottom.shape
    n = region_map.shape[0]
    groups = weight_category.shape[2] // WIDE
    tiles = weight_category.shape[2] // LANES
    field = (horizon, n, LANES)
    padded = (PAD * n, LANES)
    by_category = (horizon, tiles, LANES)
    scal = (2, LANES)
    values = pltpu.VMEM((groups * PAD, WIDE), jnp.float32)

    x = base_bottom.reshape(field)
    diag = weight_bottom.reshape(field)
    (sent,) = call(
        pack_body,
        [(n * horizon, LANES)],
        [pltpu.VMEM(field, jnp.float32), pltpu.SemaphoreType.DMA],
        (x,),
        [HBM],
        True,
    )
    got = exchange(sent, n)
    arguments = (
        x,
        base_category.reshape(by_category),
        weight_category.reshape(by_category),
        jnp.transpose(base_region, (1, 0, 2)),
        jnp.transpose(weight_region, (1, 0, 2)),
        category_map.reshape(n, LANES),
        region_map.reshape(1, n),
    )
    held = [pltpu.VMEM(arguments[i].shape, arguments[i].dtype) for i in (0, 1, 2, 3, 4, 6)]
    spread, wcat, wstore, bstore, same, table, group, cats = call(
        prepare_body,
        [
            field,
            (groups * PAD, WIDE),
            field,
            field,
            jax.ShapeDtypeStruct((n, n), jnp.bfloat16),
            jax.ShapeDtypeStruct((skus, WIDE), jnp.bfloat16),
            jax.ShapeDtypeStruct((PAD, skus), jnp.bfloat16),
            jax.ShapeDtypeStruct((n, LANES), jnp.int32),
        ],
        [
            pltpu.VMEM(padded, jnp.float32),
            values,
            *held,
            pltpu.SemaphoreType.DMA((len(arguments),)),
        ],
        arguments,
        [HBM] * len(arguments),
    )
    reg, sent = call(
        region_start_body,
        [field, (n * 2 * horizon, LANES)],
        [],
        (got, spread, wstore, bstore, same),
    )
    got = exchange(sent, n)
    fixed = (diag, wcat, wstore, table, group, cats, same)
    both = (n * (2 * horizon + 1), LANES)
    work = [values, pltpu.VMEM(padded, jnp.float32)]
    sums = (groups * PAD, WIDE)
    r, rs, cr, a, reg, sent = call(
        first_body, [field, field, sums, field, field, both], work, (spread, reg, got) + fixed
    )
    got = exchange(sent, n)
    p = r
    x, r, rs, s, ss, cr, cs, scalars, a, reg, sent = call(
        second_body,
        [field, field, field, field, field, sums, sums, scal, field, field, both],
        work,
        (a, reg, got, x, r, rs, cr) + fixed,
    )
    got = exchange(sent, n)
    x, r, p, s, scalars, a, sent = call(
        third_body,
        [field, field, field, field, scal, field, (n * (horizon + 1), LANES)],
        work + [pltpu.VMEM(field, jnp.float32)],
        (a, reg, got, x, r, rs, p, s, ss, cr, cs, scalars) + fixed,
    )
    got = exchange(sent, n)
    x, r = call(last_body, [field, field], [], (a, got, x, r, p, s, scalars))
    return x.reshape(base_bottom.shape), r.reshape(base_bottom.shape)


def week_rows(tiles, n, regions):
    sizes = (n, n, tiles, tiles, regions, regions)
    return [sum(sizes[:i]) for i in range(len(sizes) + 1)]


def week_pack_body(*refs):
    sources, out, sems = refs[:-2], refs[-2], refs[-1]
    horizon = sources[0].shape[0]
    copies, start = [], 0
    for i, source in enumerate(sources):
        rows = source.shape[1]
        target = out.at[pl.ds(0, horizon), pl.ds(start, rows)]
        copies.append(pltpu.make_async_copy(source, target, sems.at[i]))
        start += rows
    for copy in copies:
        copy.start()
    for copy in copies:
        copy.wait()


def week_table_body(
    map_ref, cats_ref, table_out, flipped_out, group_out, same_out, region_out, regions
):
    n = cats_ref.shape[0]
    lane = lax.broadcasted_iota(jnp.int32, (n, LANES), 1)
    line = lax.broadcasted_iota(jnp.int32, (n, LANES), 0)
    across = jnp.zeros((n, LANES), jnp.int32)
    down = jnp.zeros((n, LANES), jnp.int32)
    for s in range(n):
        across = jnp.where(lane % n == s, map_ref[s], across)
        down = jnp.where(line == s, map_ref[s], down)
    same_out[...] = jnp.where(across == down, 1.0, 0.0).astype(jnp.bfloat16)
    region_out[...] = jnp.where(lane % regions == down, 1.0, 0.0).astype(jnp.bfloat16)
    square = jnp.concatenate([cats_ref[...].astype(jnp.float32)] * (LANES // min(n, LANES)), axis=0)
    labels = lax.broadcasted_iota(jnp.int32, (LANES, WIDE), 1)
    downward = lax.broadcasted_iota(jnp.int32, (WIDE, LANES), 0)
    columns = [
        jnp.transpose(square[i : i + LANES]).astype(jnp.int32) & (WIDE - 1)
        for i in range(0, square.shape[0], LANES)
    ]
    for j in range(n):
        column = jnp.broadcast_to(columns[j // LANES][:, j % LANES : j % LANES + 1], (LANES, WIDE))
        table_out[j * LANES : (j + 1) * LANES, :] = jnp.where(
            column == labels, 1.0, 0.0
        ).astype(jnp.bfloat16)
        flipped_out[:, j * LANES : (j + 1) * LANES] = jnp.where(
            (cats_ref[j : j + 1, :] & (WIDE - 1)) == downward, 1.0, 0.0
        ).astype(jnp.bfloat16)
        group = cats_ref[j : j + 1, :] >> (WIDE.bit_length() - 1)
        group = jnp.broadcast_to(group, (group_out.shape[0], LANES))
        group_out[:, j * LANES : (j + 1) * LANES] = group.astype(jnp.float32).astype(jnp.bfloat16)


def ratio(top, bottom):
    return jnp.where(bottom > 0.0, top / bottom, 0.0)


def whole_sum(part):
    total = jnp.sum(jnp.sum(part, axis=0, keepdims=True), axis=1, keepdims=True)
    return jnp.broadcast_to(total, (1, LANES))


def week_body(
    core_ref, place_ref, own_ref, other_ref, table_ref, flipped_ref, group_ref, same_ref, region_ref,
    cats_ref, kept_out, line_out,
    base, basis, diag, wstore, bstore, wcat, bcat, raw_weight, raw_base, held,
    side,
):
    core = core_ref[0]
    n, skus = base.shape
    per = own_ref.shape[0] // line_out.shape[0]
    regions = raw_weight.shape[0]
    tiles = wcat.shape[0] // n * (WIDE // LANES)
    starts = week_rows(tiles, n, regions)
    chunk = min(skus, 8 * LANES)
    chunks = [slice(c, c + chunk) for c in range(0, skus, chunk)]
    for ref, c in ((own_ref, core), (other_ref, 1 - core)):
        for x in range(n // (CORES * side)):
            for t in range(0, side, 8):
                first = (x * side + t) * per
                top = pl.multiple_of(x * CORES * side + c * side + t, 8)

                def rows(row):
                    return ref[pl.ds(first + row, 8, stride=per), :]

                for j in range(n):
                    lanes = slice(j * LANES, (j + 1) * LANES)
                    base[pl.ds(top, 8), lanes] = rows(starts[0] + j)
                    diag[pl.ds(top, 8), lanes] = rows(starts[1] + j)
                for g in range(tiles):
                    lane = g * LANES % WIDE
                    down = pl.multiple_of(g * LANES // WIDE * n + top, 8)
                    wcat[pl.ds(down, 8), lane : lane + LANES] = rows(starts[2] + g)
                    bcat[pl.ds(down, 8), lane : lane + LANES] = rows(starts[3] + g)
            for k in range(side):
                first = (x * side + k) * per
                j = x * CORES * side + c * side + k
                lanes = pl.ds(pl.multiple_of(j * LANES, LANES), LANES)
                raw_base[:, lanes] = ref[first + starts[4] : first + starts[5], :]
                raw_weight[:, lanes] = ref[first + starts[5] : first + starts[6], :]

    region_table = region_ref[:, : 3 * regions]
    same = same_ref[:, : 2 * n]
    for source, target in ((raw_weight, wstore), (raw_base, bstore)):
        for lanes in chunks:
            parts = jnp.concatenate(split_all(source[:, lanes]), axis=0)
            target[:, lanes] = product(region_table, parts, ((1,), (0,)))

    def by_category(field):
        rows = wcat.shape[0]
        total = None
        for lanes in chunks:
            group = group_ref[:, lanes]
            masks = [group == g for g in range(rows // n)]
            none = jnp.zeros(group.shape, jnp.bfloat16)
            spread = jnp.concatenate(
                [jnp.where(mask, part, none) for part in split(field[:, lanes]) for mask in masks],
                axis=0,
            )
            part = product(spread, table_ref[lanes, :], ((1,), (0,)))
            total = part if total is None else total + part
        return total[:rows] + total[rows:]

    def spread(values, m, put):
        parts = jnp.concatenate(split(values), axis=0)
        groups = values.shape[0] // m
        for lanes in chunks:
            found = product(parts, flipped_ref[:, lanes], ((1,), (0,)))
            for t in range(0, chunk, LANES):
                tile = slice(lanes.start + t, lanes.start + t + LANES)
                members = cats_ref[tile.start // LANES : tile.start // LANES + 1, :]
                group = jnp.broadcast_to(members >> (WIDE.bit_length() - 1), (m, LANES))
                high, low = found[: groups * m, t : t + LANES], found[groups * m :, t : t + LANES]
                one = [
                    high[g * m : (g + 1) * m] + low[g * m : (g + 1) * m] for g in range(groups)
                ]
                bit = 1
                while len(one) > 1:
                    odd = group & bit != 0
                    pairs = [one[i : i + 2] for i in range(0, len(one), 2)]
                    one = [jnp.where(odd, *pair[::-1]) if len(pair) == 2 else pair[0] for pair in pairs]
                    bit *= 2
                put(tile, one[0])

    def by_region(part):
        return product(same, jnp.concatenate(split(part), axis=0), ((1,), (0,)))

    def tiles_in(lanes):
        for t in range(0, chunk, LANES):
            yield slice(lanes.start + t, lanes.start + t + LANES), slice(t, t + LANES)

    zero = jnp.zeros((n, LANES), jnp.float32)
    for lanes in chunks:
        sums = by_region(base[:, lanes])
        for tile, inner in tiles_in(lanes):
            basis[0, :, tile] = wstore[:, tile] * (bstore[:, tile] - sums[:, inner])
    norm = [zero]

    def start(tile, value):
        result = basis[0, :, tile] + value
        basis[0, :, tile] = result
        norm[0] = norm[0] + result * result

    spread(wcat[...] * (bcat[...] - by_category(base)), n, start)
    norms, quotients = [whole_sum(norm[0])], []
    for k in range(3):
        field, image = basis.at[k], basis.at[k + 1]
        sums = by_category(field)
        values = wcat[...] * sums
        square = values * sums
        dot = zero
        for lane in range(0, WIDE, LANES):
            for g in range(0, square.shape[0], n):
                dot = dot + square[g : g + n, lane : lane + LANES]
        for lanes in chunks:
            sums = by_region(field[:, lanes])
            for tile, inner in tiles_in(lanes):
                part = field[:, tile]
                result = diag[:, tile] * part + wstore[:, tile] * sums[:, inner]
                image[:, tile] = result
                dot = dot + part * result
        quotients.append(ratio(whole_sum(dot), norms[k]))
        back = ratio(norms[k], norms[k - 1]) if k else None
        if k == 2:
            break
        norm = [zero]

        def step(tile, value):
            result = image[:, tile] + value - quotients[k] * field[:, tile]
            if k:
                result = result - back * basis[k - 1, :, tile]
            image[:, tile] = result
            norm[0] = norm[0] + result * result

        spread(values, n, step)
        norms.append(whole_sum(norm[0]))

    lane = lax.broadcasted_iota(jnp.int32, line_out.shape, 1)
    place = lax.broadcasted_iota(jnp.int32, line_out.shape, 0)
    line = jnp.where((lane == 6) & (place == place_ref[0]), 1.0, 0.0)
    for i, value in enumerate(norms + quotients):
        line = jnp.where(lane == i, jnp.broadcast_to(value, line.shape), line)
    line_out[...] = line

    held[...] = values
    weeks = line_out.shape[0]
    tops = [
        pl.multiple_of(x * CORES * side + core * side + t, 8)
        for x in range(n // (CORES * side))
        for t in range(0, side, 8)
    ]
    for i, top in enumerate(tops):
        kept_out[4, i * 8 : i * 8 + 8, :] = base[pl.ds(top, 8), :]
        for k in range(4):
            kept_out[k, i * 8 : i * 8 + 8, :] = basis[k, pl.ds(top, 8), :]
    mine = jnp.concatenate(
        [held[pl.ds(g + top, 8), :] for g in range(0, held.shape[0], n) for top in tops], axis=0
    )

    def finish(tile, value):
        result = kept_out[3, :, tile] + value - quotients[2] * kept_out[2, :, tile]
        kept_out[3, :, tile] = result - back * kept_out[1, :, tile]

    spread(mine, weeks, finish)


def week_combine_body(lines_ref, kept_ref, send_ref, horizon):
    weeks = lines_ref.shape[0]
    n = kept_ref.shape[2] // LANES
    week = lax.broadcasted_iota(jnp.int32, (weeks, LANES), 0)
    lines = jnp.where(week < horizon, lines_ref[...], 0.0)
    n1, n2, n3, a1, a2, a3, mark = [
        jnp.take_along_axis(lines, jnp.full((weeks, LANES), i, jnp.int32), axis=1) for i in range(7)
    ]
    e2, e3 = ratio(n2, n1), ratio(n3, n2)

    def dot(left, right):
        terms = n1 * left[0] * right[0] + n2 * left[1] * right[1] + n3 * left[2] * right[2]
        return jnp.sum(terms, axis=0, keepdims=True)

    zero = jnp.zeros((weeks, LANES), jnp.float32)
    x = [zero, zero, zero]
    r = [zero + 1.0, zero, zero, zero]
    p = r[:3]
    rr = dot(r, r)
    for k in range(3):
        image = [
            a1 * p[0] + e2 * p[1],
            p[0] + a2 * p[1] + e3 * p[2],
            p[1] + a3 * p[2],
            p[2],
        ]
        alpha = rr / dot(p, image)
        x = [left + alpha * right for left, right in zip(x, p)]
        r = [left - alpha * right for left, right in zip(r, image)]
        if k < 2:
            new = dot(r, r)
            p = [left + new / rr * right for left, right in zip(r[:3], p)]
            rr = new
    mine = mark > 0.0
    x = [jnp.sum(jnp.where(mine, value, 0.0), axis=0, keepdims=True) for value in x]
    r = [jnp.sum(jnp.where(mine, value, 0.0), axis=0, keepdims=True) for value in r]
    rows = send_ref.shape[0] // weeks
    for t in range(0, weeks, 8):
        for j in range(n):
            lanes = slice(j * LANES, (j + 1) * LANES)
            parts = [kept_ref[k, t : t + 8, lanes] for k in range(4)]
            left = kept_ref[4, t : t + 8, lanes]
            right = r[3] * parts[3]
            for k in range(3):
                left = left + x[k] * parts[k]
                right = right + r[k] * parts[k]
            first = t * rows + j
            send_ref[pl.ds(first, 8, stride=rows), :] = left
            send_ref[pl.ds(first + n, 8, stride=rows), :] = right


def week_last_body(got_ref, x_out, r_out, sems):
    horizon, n, _ = x_out.shape
    copies = [
        pltpu.make_async_copy(
            got_ref.at[pl.ds(0, horizon), pl.ds(i * n, n)], target, sems.at[i]
        )
        for i, target in enumerate((x_out, r_out))
    ]
    for copy in copies:
        copy.start()
    for copy in copies:
        copy.wait()


def exchange_weeks(blocks):
    return lax.all_to_all(blocks, ("x", "sku"), split_axis=0, concat_axis=0, tiled=True)


def by_weeks(
    base_bottom,
    weight_bottom,
    base_category,
    weight_category,
    base_region,
    weight_region,
    category_map,
    region_map,
):
    stores, horizon, skus = base_bottom.shape
    n = region_map.shape[0]
    regions = weight_region.shape[0]
    tiles = weight_category.shape[2] // LANES
    groups = weight_category.shape[2] // WIDE
    side = lax.axis_size("sku")
    weeks = lax.axis_size("x") * side
    place = lax.axis_index("x") * side + lax.axis_index("sku")
    place = place.astype(jnp.int32).reshape(1)
    core = lax.axis_index("core").astype(jnp.int32).reshape(1)
    cats = category_map.reshape(n, LANES)
    sources = (
        base_bottom.reshape(horizon, n, LANES),
        weight_bottom.reshape(horizon, n, LANES),
        weight_category.reshape(horizon, tiles, LANES),
        base_category.reshape(horizon, tiles, LANES),
        jnp.transpose(base_region, (1, 0, 2)),
        jnp.transpose(weight_region, (1, 0, 2)),
    )
    per = week_rows(tiles, n, regions)[-1]
    (sent,) = call(
        week_pack_body,
        [(weeks, per, LANES)],
        [pltpu.SemaphoreType.DMA((len(sources),))],
        sources,
        [HBM] * len(sources),
        out_specs=(HBM,),
    )
    own = exchange_weeks(sent)
    other = lax.ppermute(own, "core", [(0, 1), (1, 0)])
    table, flipped, group, same, region = call(
        lambda *refs: week_table_body(*refs, regions),
        [
            jax.ShapeDtypeStruct((skus, WIDE), jnp.bfloat16),
            jax.ShapeDtypeStruct((WIDE, skus), jnp.bfloat16),
            jax.ShapeDtypeStruct((n, skus), jnp.bfloat16),
            jax.ShapeDtypeStruct((n, LANES), jnp.bfloat16),
            jax.ShapeDtypeStruct((n, LANES), jnp.bfloat16),
        ],
        [],
        (region_map, cats),
        [SMEM, VMEM],
    )
    full = pltpu.VMEM((n, skus), jnp.float32)
    raw = pltpu.VMEM((regions, skus), jnp.float32)
    cat = pltpu.VMEM((groups * n, WIDE), jnp.float32)
    kept, line = call(
        lambda *refs: week_body(*refs, side),
        [(5, weeks, skus), (weeks, LANES)],
        [
            full, pltpu.VMEM((4, n, skus), jnp.float32),
            full, full, full, cat, cat, raw, raw, cat,
        ],
        (
            core, place, own.reshape(-1, LANES), other.reshape(-1, LANES),
            table, flipped, group, same, region, cats,
        ),
        [SMEM, SMEM, VMEM, FREE] + [VMEM] * 6,
    )
    lines = exchange_weeks(line.reshape(weeks, 1, LANES)).reshape(weeks, LANES)
    (sent,) = call(
        lambda *refs: week_combine_body(*refs, horizon),
        [(weeks * 2 * n, LANES)],
        [],
        (lines, kept),
        [VMEM] * 2,
    )
    got = exchange_weeks(sent.reshape(weeks, 2 * n, LANES))
    x, r = call(
        week_last_body,
        [(horizon, n, LANES)] * 2,
        [pltpu.SemaphoreType.DMA((2,))],
        (got,),
        [VMEM],
        out_specs=(HBM, HBM),
    )
    return x.reshape(base_bottom.shape), r.reshape(base_bottom.shape)


def solution(mesh):
    def mapped(device_mesh, body, stores):
        split_stores = P(stores, None, None)
        split_skus = P(None, None, stores)
        return jax.shard_map(
            body,
            mesh=device_mesh,
            in_specs=(split_stores,) * 4 + (split_skus,) * 2 + (P(), P()),
            out_specs=(split_stores,) * 2,
            check_vma=False,
        )

    side = mesh.shape["sku"]
    chips = mesh.devices.reshape(-1, CORES, side)

    def program(base_bottom, *others):
        stores, horizon, skus = base_bottom.shape
        fits = 16 * stores * skus * 4 <= 16 << 20
        fits = fits and 3 * others[3].shape[0] <= LANES and LANES % stores == 0
        if fits and horizon <= chips.shape[0] * side and side % 8 == 0:
            device_mesh = Mesh(chips, ("x", "core", "sku"))
            return mapped(device_mesh, by_weeks, ("x", "core", "sku"))(base_bottom, *others)
        return mapped(mesh, on_device, ("store", "sku"))(base_bottom, *others)

    return program
```

profile of v0, /device:TPU:0, one launch (start us, length us, event | category | flops | bytes accessed | tf_op | source)
XLA Modules:
  0.0 78.9 jit_solution(6734832618036322063)
XLA Ops:
  0.6 1.3 %shard_map.95 = f32[16,144,128]{2,1,0:T(8,128)S(1)} custom-call(f32[13,32,128]{2,1,0:T(8,128)} %bitcast.25, f32[13,32,128]{2,1,0:T(8,128)} %bitcast.26, f32[13,8,128]{2,1,0:T(8,128)} %bitcast.29, f32[13,8,128]{2,1,0:T(8,128)} %bitcast.30, f32[13,32,128]{2,1,0:T(8,128)} %bitcast.27, f32[13,32,128]{2,1,0:T(8,128)} %bitcast.28), custom_call_target="tpu_custom_call" | custom-call | tf_op jit(solution)/shard_map/pallas_call | solution.py:36
  2.0 0.0 copy-start
  2.0 0.0 copy-start.1
  2.0 38.1 %all_to_all.15 = f32[16,144,128]{2,1,0:T(8,128)S(1)} all-to-all(f32[16,144,128]{2,1,0:T(8,128)S(1)} %shard_map.95), channel_id=1, replica_groups=mesh['x'=2,'core'=2,'sku'=8] {'x','sku'}, dimensions={0} | all-to-all | bytes 2359296 | tf_op jit(solution)/shard_map/all_to_all | solution.py:799
  40.1 0.0 collective-permute-start
  40.1 0.0 copy-done
  40.1 0.0 copy-done.1
  40.1 2.2 %shard_map.96 = (bf16[4096,256]{1,0:T(8,128)(2,1)S(1)}, bf16[256,4096]{1,0:T(8,128)(2,1)S(1)}, bf16[32,4096]{1,0:T(8,128)(2,1)S(1)}, bf16[32,128]{1,0:T(8,128)(2,1)S(1)}, bf16[32,128]{1,0:T(8,128)(2,1)S(1)}) custom-call(s32[32]{0:T(128)S(1)} %copy-done.1, s32[32,128]{1,0:T(8,128)S(1)} %bitcast.21), custom_call_target="tpu_custom_call" | custom-call | tf_op jit(solution)/shard_map/pallas_call | solution.py:36
  42.3 0.6 collective-permute-done
  42.9 7.4 %shard_map.97 = (f32[5,16,4096]{2,1,0:T(8,128)S(1)}, f32[16,128]{1,0:T(8,128)S(1)}) custom-call(s32[1]{0:T(128)} %bitcast.refs_0_, s32[1]{0:T(128)} %bitcast.1.refs_1_, f32[2304,128]{1,0:T(8,128)S(1)} %bitcast.18, f32[2304,128]{1,0:T(8,128)S(1)} %bitcast.20, bf16[4096,256]{1,0:T(8,128)(2,1)S(1)} %get-tuple-element.11.refs_4_, ...), custom_call_target="tpu_custom_call" | custom-call | tf_op jit(solution)/shard_map/pallas_call | solution.py:36
  50.3 10.1 %all_to_all.16 = f32[16,1,128]{2,1,0:T(1,128)S(1)} all-to-all(f32[16,1,128]{2,1,0:T(1,128)S(1)} %bitcast.24), channel_id=1, replica_groups=mesh['x'=2,'core'=2,'sku'=8] {'x','sku'}, dimensions={0} | all-to-all | bytes 16384 | tf_op jit(solution)/shard_map/all_to_all | solution.py:799
  60.4 0.6 shard_map.98
  61.0 17.0 %all_to_all.17.got_ref = f32[16,64,128]{2,1,0:T(8,128)S(1)} all-to-all(f32[16,64,128]{2,1,0:T(8,128)S(1)} %bitcast.19), channel_id=1, replica_groups=mesh['x'=2,'core'=2,'sku'=8] {'x','sku'}, dimensions={0} | all-to-all | bytes 1048576 | tf_op jit(solution)/shard_map/all_to_all | solution.py:799
  78.1 0.8 shard_map.99
Async XLA Ops:
  2.0 38.1 %copy-start = (s32[4096]{0:T(1024)S(1)}, s32[4096]{0:T(1024)}, u32[]{:S(2)}) copy-start(s32[4096]{0:T(1024)} %param.14) | copy-start | bytes 49156
  2.0 38.1 %copy-start.1 = (s32[32]{0:T(128)S(1)}, s32[32]{0:T(128)}, u32[]{:S(2)}) copy-start(s32[32]{0:T(128)} %refs_0_.1) | copy-start | bytes 388
  40.1 2.8 %collective-permute-start = (f32[16,144,128]{2,1,0:T(8,128)S(1)}, f32[16,144,128]{2,1,0:T(8,128)S(1)}, u32[]{:S(2)}, u32[]{:S(2)}) collective-permute-start(f32[16,144,128]{2,1,0:T(8,128)S(1)} %all_to_all.15), channel_id=1, source_target_pairs={{0,8},{8,0},{1,9},{9,1},{2,10},{10,2},{3,11},{11,3},{4,12},{12,4},... | collective-permute-start | bytes 3538952 | tf_op jit(solution)/shard_map/ppermute | solution.py:841
where the time goes:
time: 79.1 us; the launch traced here: 78.9 us
  blocking collectives  65.2 us (82%)
  Pallas kernels  12.3 us (16%)
    all_to_all x3, blocking collectives, exchange_weeks(): lax.all_to_all(blocks, ('x', 'sku'), split_axis=0, concat_axis=0, tiled=T...  65.2 us
    pallas_call x5, Pallas kernels, call(): pl.pallas_call(body, out_shape=tuple((pltpu.VMEM(out.shape, out.dtype) if...  12.3 us
  transfers between devices with their start and end apart: 1, of which 1 were waited for; matrix products, arithmetic and copies ran while one was open for 0% of the time, Pallas kernels for 3%

commit v1 on v0

--- a/solution.py
+++ b/solution.py
@@ -578,7 +578,7 @@
     regions = raw_weight.shape[0]
     tiles = wcat.shape[0] // n * (WIDE // LANES)
     starts = week_rows(tiles, n, regions)
-    chunk = min(skus, 8 * LANES)
+    chunk = skus
     chunks = [slice(c, c + chunk) for c in range(0, skus, chunk)]
     for ref, c in ((own_ref, core), (other_ref, 1 - core)):
         for x in range(n // (CORES * side)):
@@ -614,17 +614,13 @@
 
     def by_category(field):
         rows = wcat.shape[0]
-        total = None
-        for lanes in chunks:
-            group = group_ref[:, lanes]
-            masks = [group == g for g in range(rows // n)]
-            none = jnp.zeros(group.shape, jnp.bfloat16)
-            spread = jnp.concatenate(
-                [jnp.where(mask, part, none) for part in split(field[:, lanes]) for mask in masks],
-                axis=0,
-            )
-            part = product(spread, table_ref[lanes, :], ((1,), (0,)))
-            total = part if total is None else total + part
+        group = group_ref[...]
+        masks = [group == g for g in range(rows // n)]
+        none = jnp.zeros(group.shape, jnp.bfloat16)
+        spread = jnp.concatenate(
+            [jnp.where(mask, part, none) for part in split(field[...]) for mask in masks], axis=0
+        )
+        total = product(spread, table_ref[...], ((1,), (0,)))
         return total[:rows] + total[rows:]
 
     def spread(values, m, put):

time: 79.1 us -> 78.4 us (level)
  no operation moved by 1% of the time
where the time goes in v1:
time: 78.4 us; the launch traced here: 78.1 us
  blocking collectives  65.2 us (83%)
  Pallas kernels  11.6 us (15%)
    all_to_all x3, blocking collectives, exchange_weeks(): lax.all_to_all(blocks, ('x', 'sku'), split_axis=0, concat_axis=0, tiled=T...  65.2 us
    pallas_call x5, Pallas kernels, call(): pl.pallas_call(body, out_shape=tuple((pltpu.VMEM(out.shape, out.dtype) if...  11.6 us
  transfers between devices with their start and end apart: 1, of which 1 were waited for; matrix products, arithmetic and copies ran while one was open for 0% of the time, Pallas kernels for 3%

profile of v1, /device:TPU:0, one launch (start us, length us, event | category | flops | bytes accessed | tf_op | source)
XLA Modules:
  0.0 78.1 jit_solution(15955671583691161363)
XLA Ops:
  0.6 1.3 %shard_map.95 = f32[16,144,128]{2,1,0:T(8,128)S(1)} custom-call(f32[13,32,128]{2,1,0:T(8,128)} %bitcast.25, f32[13,32,128]{2,1,0:T(8,128)} %bitcast.26, f32[13,8,128]{2,1,0:T(8,128)} %bitcast.29, f32[13,8,128]{2,1,0:T(8,128)} %bitcast.30, f32[13,32,128]{2,1,0:T(8,128)} %bitcast.27, f32[13,32,128]{2,1,0:T(8,128)} %bitcast.28), custom_call_target="tpu_custom_call" | custom-call | tf_op jit(solution)/shard_map/pallas_call | solution.py:36
  2.0 0.0 copy-start
  2.0 0.0 copy-start.1
  2.0 38.1 %all_to_all.15 = f32[16,144,128]{2,1,0:T(8,128)S(1)} all-to-all(f32[16,144,128]{2,1,0:T(8,128)S(1)} %shard_map.95), channel_id=1, replica_groups=mesh['x'=2,'core'=2,'sku'=8] {'x','sku'}, dimensions={0} | all-to-all | bytes 2359296 | tf_op jit(solution)/shard_map/all_to_all | solution.py:795
  40.1 0.0 collective-permute-start
  40.1 0.0 copy-done
  40.1 0.0 copy-done.1
  40.1 2.2 %shard_map.96 = (bf16[4096,256]{1,0:T(8,128)(2,1)S(1)}, bf16[256,4096]{1,0:T(8,128)(2,1)S(1)}, bf16[32,4096]{1,0:T(8,128)(2,1)S(1)}, bf16[32,128]{1,0:T(8,128)(2,1)S(1)}, bf16[32,128]{1,0:T(8,128)(2,1)S(1)}) custom-call(s32[32]{0:T(128)S(1)} %copy-done.1, s32[32,128]{1,0:T(8,128)S(1)} %bitcast.21), custom_call_target="tpu_custom_call" | custom-call | tf_op jit(solution)/shard_map/pallas_call | solution.py:36
  42.3 0.6 collective-permute-done
  42.9 6.7 %shard_map.97 = (f32[5,16,4096]{2,1,0:T(8,128)S(1)}, f32[16,128]{1,0:T(8,128)S(1)}) custom-call(s32[1]{0:T(128)} %bitcast.refs_0_, s32[1]{0:T(128)} %bitcast.1.refs_1_, f32[2304,128]{1,0:T(8,128)S(1)} %bitcast.18, f32[2304,128]{1,0:T(8,128)S(1)} %bitcast.20, bf16[4096,256]{1,0:T(8,128)(2,1)S(1)} %get-tuple-element.11.refs_4_, ...), custom_call_target="tpu_custom_call" | custom-call | tf_op jit(solution)/shard_map/pallas_call | solution.py:36
  49.6 10.1 %all_to_all.16 = f32[16,1,128]{2,1,0:T(1,128)S(1)} all-to-all(f32[16,1,128]{2,1,0:T(1,128)S(1)} %bitcast.24), channel_id=1, replica_groups=mesh['x'=2,'core'=2,'sku'=8] {'x','sku'}, dimensions={0} | all-to-all | bytes 16384 | tf_op jit(solution)/shard_map/all_to_all | solution.py:795
  59.7 0.6 shard_map.98
  60.3 17.0 %all_to_all.17.got_ref = f32[16,64,128]{2,1,0:T(8,128)S(1)} all-to-all(f32[16,64,128]{2,1,0:T(8,128)S(1)} %bitcast.19), channel_id=1, replica_groups=mesh['x'=2,'core'=2,'sku'=8] {'x','sku'}, dimensions={0} | all-to-all | bytes 1048576 | tf_op jit(solution)/shard_map/all_to_all | solution.py:795
  77.4 0.8 shard_map.99
Async XLA Ops:
  2.0 38.1 %copy-start = (s32[4096]{0:T(1024)S(1)}, s32[4096]{0:T(1024)}, u32[]{:S(2)}) copy-start(s32[4096]{0:T(1024)} %param.14) | copy-start | bytes 49156
  2.0 38.1 %copy-start.1 = (s32[32]{0:T(128)S(1)}, s32[32]{0:T(128)}, u32[]{:S(2)}) copy-start(s32[32]{0:T(128)} %refs_0_.1) | copy-start | bytes 388
  40.1 2.8 %collective-permute-start = (f32[16,144,128]{2,1,0:T(8,128)S(1)}, f32[16,144,128]{2,1,0:T(8,128)S(1)}, u32[]{:S(2)}, u32[]{:S(2)}) collective-permute-start(f32[16,144,128]{2,1,0:T(8,128)S(1)} %all_to_all.15), channel_id=1, source_target_pairs={{0,8},{8,0},{1,9},{9,1},{2,10},{10,2},{3,11},{11,3},{4,12},{12,4},... | collective-permute-start | bytes 3538952 | tf_op jit(solution)/shard_map/ppermute | solution.py:837

commit v2 on v1

--- a/solution.py
+++ b/solution.py
@@ -14,6 +14,7 @@
 SMEM = pl.BlockSpec(memory_space=pltpu.SMEM)
 FREE = pl.BlockSpec(memory_space=pltpu.VMEM)
 CORES = 2
+CUTS = 4
 
 
 def exchange(blocks, n):
@@ -509,14 +510,21 @@
     return [sum(sizes[:i]) for i in range(len(sizes) + 1)]
 
 
+def week_cuts(horizon):
+    ends = [horizon * i // CUTS for i in range(CUTS + 1)]
+    return [(a, b - a) for a, b in zip(ends, ends[1:]) if b > a]
+
+
 def week_pack_body(*refs):
     sources, out, sems = refs[:-2], refs[-2], refs[-1]
     horizon = sources[0].shape[0]
     copies, start = [], 0
-    for i, source in enumerate(sources):
+    for source in sources:
         rows = source.shape[1]
-        target = out.at[pl.ds(0, horizon), pl.ds(start, rows)]
-        copies.append(pltpu.make_async_copy(source, target, sems.at[i]))
+        for first, number in week_cuts(horizon):
+            weeks = pl.ds(first, number)
+            target = out.at[weeks, pl.ds(start, rows)]
+            copies.append(pltpu.make_async_copy(source.at[weeks], target, sems.at[len(copies)]))
         start += rows
     for copy in copies:
         copy.start()
@@ -779,12 +787,12 @@
 
 def week_last_body(got_ref, x_out, r_out, sems):
     horizon, n, _ = x_out.shape
-    copies = [
-        pltpu.make_async_copy(
-            got_ref.at[pl.ds(0, horizon), pl.ds(i * n, n)], target, sems.at[i]
-        )
-        for i, target in enumerate((x_out, r_out))
-    ]
+    copies = []
+    for i, target in enumerate((x_out, r_out)):
+        for first, number in week_cuts(horizon):
+            weeks = pl.ds(first, number)
+            source = got_ref.at[weeks, pl.ds(i * n, n)]
+            copies.append(pltpu.make_async_copy(source, target.at[weeks], sems.at[len(copies)]))
     for copy in copies:
         copy.start()
     for copy in copies:
@@ -828,7 +836,7 @@
     (sent,) = call(
         week_pack_body,
         [(weeks, per, LANES)],
-        [pltpu.SemaphoreType.DMA((len(sources),))],
+        [pltpu.SemaphoreType.DMA((CUTS * len(sources),))],
         sources,
         [HBM] * len(sources),
         out_specs=(HBM,),
@@ -876,7 +884,7 @@
     x, r = call(
         week_last_body,
         [(horizon, n, LANES)] * 2,
-        [pltpu.SemaphoreType.DMA((2,))],
+        [pltpu.SemaphoreType.DMA((2 * CUTS,))],
         (got,),
         [VMEM],
         out_specs=(HBM, HBM),

time: 78.4 us -> 78.6 us (level)
  no operation moved by 1% of the time
where the time goes in v2:
time: 78.6 us; the launch traced here: 78.3 us
  blocking collectives  65.2 us (83%)
  Pallas kernels  11.8 us (15%)
    all_to_all x3, blocking collectives, exchange_weeks(): lax.all_to_all(blocks, ('x', 'sku'), split_axis=0, concat_axis=0, tiled=T...  65.2 us
    pallas_call x5, Pallas kernels, call(): pl.pallas_call(body, out_shape=tuple((pltpu.VMEM(out.shape, out.dtype) if...  11.8 us
  transfers between devices with their start and end apart: 1, of which 1 were waited for; matrix products, arithmetic and copies ran while one was open for 0% of the time, Pallas kernels for 3%

profile of v2, /device:TPU:0, one launch (start us, length us, event | category | flops | bytes accessed | tf_op | source)
XLA Modules:
  0.0 78.3 jit_solution(3248913478717067910)
XLA Ops:
  0.6 1.4 %shard_map.95 = f32[16,144,128]{2,1,0:T(8,128)S(1)} custom-call(f32[13,32,128]{2,1,0:T(8,128)} %bitcast.25, f32[13,32,128]{2,1,0:T(8,128)} %bitcast.26, f32[13,8,128]{2,1,0:T(8,128)} %bitcast.29, f32[13,8,128]{2,1,0:T(8,128)} %bitcast.30, f32[13,32,128]{2,1,0:T(8,128)} %bitcast.27, f32[13,32,128]{2,1,0:T(8,128)} %bitcast.28), custom_call_target="tpu_custom_call" | custom-call | tf_op jit(solution)/shard_map/pallas_call | solution.py:37
  2.1 0.0 copy-start
  2.1 0.0 copy-start.1
  2.1 38.1 %all_to_all.15 = f32[16,144,128]{2,1,0:T(8,128)S(1)} all-to-all(f32[16,144,128]{2,1,0:T(8,128)S(1)} %shard_map.95), channel_id=1, replica_groups=mesh['x'=2,'core'=2,'sku'=8] {'x','sku'}, dimensions={0} | all-to-all | bytes 2359296 | tf_op jit(solution)/shard_map/all_to_all | solution.py:803
  40.2 0.0 collective-permute-start
  40.2 0.0 copy-done
  40.2 0.0 copy-done.1
  40.2 2.2 %shard_map.96 = (bf16[4096,256]{1,0:T(8,128)(2,1)S(1)}, bf16[256,4096]{1,0:T(8,128)(2,1)S(1)}, bf16[32,4096]{1,0:T(8,128)(2,1)S(1)}, bf16[32,128]{1,0:T(8,128)(2,1)S(1)}, bf16[32,128]{1,0:T(8,128)(2,1)S(1)}) custom-call(s32[32]{0:T(128)S(1)} %copy-done.1, s32[32,128]{1,0:T(8,128)S(1)} %bitcast.21), custom_call_target="tpu_custom_call" | custom-call | tf_op jit(solution)/shard_map/pallas_call | solution.py:37
  42.4 0.6 collective-permute-done
  43.0 6.7 %shard_map.97 = (f32[5,16,4096]{2,1,0:T(8,128)S(1)}, f32[16,128]{1,0:T(8,128)S(1)}) custom-call(s32[1]{0:T(128)} %bitcast.refs_0_, s32[1]{0:T(128)} %bitcast.1.refs_1_, f32[2304,128]{1,0:T(8,128)S(1)} %bitcast.18, f32[2304,128]{1,0:T(8,128)S(1)} %bitcast.20, bf16[4096,256]{1,0:T(8,128)(2,1)S(1)} %get-tuple-element.11.refs_4_, ...), custom_call_target="tpu_custom_call" | custom-call | tf_op jit(solution)/shard_map/pallas_call | solution.py:37
  49.7 10.1 %all_to_all.16 = f32[16,1,128]{2,1,0:T(1,128)S(1)} all-to-all(f32[16,1,128]{2,1,0:T(1,128)S(1)} %bitcast.24), channel_id=1, replica_groups=mesh['x'=2,'core'=2,'sku'=8] {'x','sku'}, dimensions={0} | all-to-all | bytes 16384 | tf_op jit(solution)/shard_map/all_to_all | solution.py:803
  59.8 0.6 shard_map.98
  60.4 17.0 %all_to_all.17.got_ref = f32[16,64,128]{2,1,0:T(8,128)S(1)} all-to-all(f32[16,64,128]{2,1,0:T(8,128)S(1)} %bitcast.19), channel_id=1, replica_groups=mesh['x'=2,'core'=2,'sku'=8] {'x','sku'}, dimensions={0} | all-to-all | bytes 1048576 | tf_op jit(solution)/shard_map/all_to_all | solution.py:803
  77.5 0.8 %shard_map.99 = (f32[13,32,128]{2,1,0:T(8,128)}, f32[13,32,128]{2,1,0:T(8,128)}) custom-call(f32[16,64,128]{2,1,0:T(8,128)S(1)} %all_to_all.17.got_ref), custom_call_target="tpu_custom_call" | custom-call | tf_op jit(solution)/shard_map/pallas_call | solution.py:37
Async XLA Ops:
  2.1 38.1 %copy-start = (s32[4096]{0:T(1024)S(1)}, s32[4096]{0:T(1024)}, u32[]{:S(2)}) copy-start(s32[4096]{0:T(1024)} %param.14) | copy-start | bytes 49156
  2.1 38.1 %copy-start.1 = (s32[32]{0:T(128)S(1)}, s32[32]{0:T(128)}, u32[]{:S(2)}) copy-start(s32[32]{0:T(128)} %refs_0_.1) | copy-start | bytes 388
  40.2 2.8 %collective-permute-start = (f32[16,144,128]{2,1,0:T(8,128)S(1)}, f32[16,144,128]{2,1,0:T(8,128)S(1)}, u32[]{:S(2)}, u32[]{:S(2)}) collective-permute-start(f32[16,144,128]{2,1,0:T(8,128)S(1)} %all_to_all.15), channel_id=1, source_target_pairs={{0,8},{8,0},{1,9},{9,1},{2,10},{10,2},{3,11},{11,3},{4,12},{12,4},... | collective-permute-start | bytes 3538952 | tf_op jit(solution)/shard_map/ppermute | solution.py:845
